TPU v7x, 128 devices: a whole 4x4x4 slice. The times are simulated.
128 devices in a mesh: struct: 4 (over x), fluid: 32 (over z, y, core).
Axes of the slice: x: 4, y: 4, z: 4, core: 2. Of those that a mesh axis runs over, the one named last changes fastest.
Arguments:
- shell_motion: float32 [3, 1048576], P(None, ('struct', 'fluid')), may hold values from -6 to 6
- owner: int32 [1048576, 1], P(('struct', 'fluid')), may hold values from 0 to 127; in each aligned block of 8192 rows (0 to 8191, 8192 to 16383, ...) at most 128 rows name the same one
- stencil_slot: int32 [4, 8, 256, 128], P(None, 'struct', 'fluid'), may hold values from 0 to 16383
- stencil_weight: float32 [4, 8, 256, 128], P(None, 'struct', 'fluid'), may hold values from 0 to 0.5
- prev_motion: float32 [3, 8, 256, 256], P(None, 'struct', 'fluid'), may hold values from -6 to 6
- node_offset: float32 [3, 8, 256, 256], P(None, 'struct', 'fluid'), may hold values from -0.07 to 0.07
- cell_split: int32 [8, 256, 256], P('struct', 'fluid'), may hold values from 0 to 3
Outputs:
- mesh_motion: float32 [3, 8, 256, 256], P(None, 'struct', 'fluid')
Inputs may be any that keep to these rules, and one draw needn't show every extreme that they name: Among the 8192 shell nodes of one device, no owner is named by more than 128 of them, a bound that some block reaches.
All inputs are finite; a program needn't handle non-finite values.
Results may differ from a plain program's by a relative error of at most 0.0003.
Values sent between devices are 32-bit elements; how exact they have to be, the bound alone decides.
No kernel may reach another device: no remote copies, remote signals or barrier semaphores. Data moves between devices by JAX's collectives and lax.ppermute only.
A program may use at most 64 MiB of HBM per device.

v0:
```python
from functools import reduce
import jax
import jax.numpy as jnp
from jax import lax
from jax.sharding import PartitionSpec as P

SWEEPS = 4
LAMBDA_RATIO = 1.0
RELAX_FACTOR = 0.5
STEP_ORDERS = ((0, 1, 2), (0, 2, 1), (1, 0, 2), (1, 2, 0), (2, 0, 1), (2, 1, 0))
CORNER_LIST = tuple(
    ((shift_x, shift_y, shift_z) for shift_x in (0, 1) for shift_y in (0, 1) for shift_z in (0, 1))
)


def from_behind(block, axis, distance):
    devices = range(lax.axis_size(axis))
    route = [((i - distance) % len(devices), i) for i in devices]
    return lax.ppermute(block, axis, route)


def cross_product(left_vec, right_vec):
    return jnp.stack(
        [
            left_vec[1] * right_vec[2] - left_vec[2] * right_vec[1],
            left_vec[2] * right_vec[0] - left_vec[0] * right_vec[2],
            left_vec[0] * right_vec[1] - left_vec[1] * right_vec[0],
        ]
    )


def select_flip(flip_y, flip_z, unflipped, flipped_z, flipped_y, flipped_both):
    return jnp.where(
        flip_y, jnp.where(flip_z, flipped_both, flipped_y), jnp.where(flip_z, flipped_z, unflipped)
    )


def reflect_corners(corners, flip_y, flip_z):
    result = {}
    for corner in CORNER_LIST:
        shift_x, shift_y, shift_z = corner
        result[corner] = select_flip(
            flip_y,
            flip_z,
            corners[corner],
            corners[shift_x, shift_y, 1 - shift_z],
            corners[shift_x, 1 - shift_y, shift_z],
            corners[shift_x, 1 - shift_y, 1 - shift_z],
        )
    return result


def flip_masks(split_codes):
    flip_y = split_codes // 2 == 1
    flip_z = split_codes % 2 == 1
    sign_y = jnp.where(flip_y, -1.0, 1.0).astype(jnp.float32)
    sign_z = jnp.where(flip_z, -1.0, 1.0).astype(jnp.float32)
    return (flip_y, flip_z, sign_y, sign_z)


def lattice_edge(vertex, sign_y, sign_z):
    return jnp.stack(
        [jnp.full_like(sign_y, float(vertex[0])), sign_y * vertex[1], sign_z * vertex[2]]
    )


def element_gradients(offsets, step_order, sign_y, sign_z):
    position = [0, 0, 0]
    vertex_path = [(0, 0, 0)]
    for axis_id in step_order:
        position[axis_id] = 1
        vertex_path.append(tuple(position))
    anchor = offsets[vertex_path[0]]
    edge_list = [
        lattice_edge(vertex, sign_y, sign_z) + offsets[vertex] - anchor
        for vertex in vertex_path[1:]
    ]
    across_one = cross_product(edge_list[1], edge_list[2])
    across_two = cross_product(edge_list[2], edge_list[0])
    across_three = cross_product(edge_list[0], edge_list[1])
    volume_six = jnp.sum(edge_list[0] * across_one, axis=0)
    grad_one = across_one / volume_six
    grad_two = across_two / volume_six
    grad_three = across_three / volume_six
    grad_zero = -(grad_one + grad_two + grad_three)
    return (vertex_path, [grad_zero, grad_one, grad_two, grad_three])


def element_forces(offsets, displace, sign_y, sign_z):
    forces = {corner: jnp.zeros_like(displace[corner]) for corner in CORNER_LIST}
    for step_order in STEP_ORDERS:
        vertex_path, gradient_list = element_gradients(offsets, step_order, sign_y, sign_z)
        tensor = displace[vertex_path[0]][:, None] * gradient_list[0][None, :]
        for vertex in range(1, 4):
            tensor = (
                tensor + displace[vertex_path[vertex]][:, None] * gradient_list[vertex][None, :]
            )
        trace_sum = tensor[0, 0] + tensor[1, 1] + tensor[2, 2]
        symmetric = tensor + jnp.swapaxes(tensor, 0, 1)
        for vertex in range(4):
            gradient = gradient_list[vertex]
            nodal_force = LAMBDA_RATIO * trace_sum * gradient + jnp.sum(
                symmetric * gradient[None, :], axis=1
            )
            forces[vertex_path[vertex]] = forces[vertex_path[vertex]] + nodal_force
    return forces


def element_diagonal(offsets, sign_y, sign_z):
    result = {corner: jnp.zeros_like(offsets[corner]) for corner in CORNER_LIST}
    for step_order in STEP_ORDERS:
        vertex_path, gradient_list = element_gradients(offsets, step_order, sign_y, sign_z)
        for vertex in range(4):
            gradient = gradient_list[vertex]
            entry = (LAMBDA_RATIO + 1.0) * gradient * gradient + jnp.sum(
                gradient * gradient, axis=0
            )
            result[vertex_path[vertex]] = result[vertex_path[vertex]] + entry
    return result


def cell_corners(extended, count_y, count_z):
    return {
        corner: jnp.roll(
            extended[:, corner[1] : corner[1] + count_y, corner[2] : corner[2] + count_z, :],
            -corner[0],
            axis=3,
        )
        for corner in CORNER_LIST
    }


def corner_diagonal(offset_ext, masks, count_y, count_z):
    flip_y, flip_z, sign_y, sign_z = masks
    offsets = reflect_corners(cell_corners(offset_ext, count_y, count_z), flip_y, flip_z)
    return reflect_corners(element_diagonal(offsets, sign_y, sign_z), flip_y, flip_z)


def corner_forces(offset_ext, motion_ext, masks, count_y, count_z):
    flip_y, flip_z, sign_y, sign_z = masks
    offsets = reflect_corners(cell_corners(offset_ext, count_y, count_z), flip_y, flip_z)
    displace = reflect_corners(cell_corners(motion_ext, count_y, count_z), flip_y, flip_z)
    return reflect_corners(element_forces(offsets, displace, sign_y, sign_z), flip_y, flip_z)


def spread_sum(per_corner):
    pieces = [
        jnp.roll(
            jnp.pad(
                per_corner[corner],
                ((0, 0), (corner[1], 1 - corner[1]), (corner[2], 1 - corner[2]), (0, 0)),
            ),
            corner[0],
            axis=3,
        )
        for corner in CORNER_LIST
    ]
    return reduce(jnp.add, pieces)


def upper_ghosts(nodal_field):
    top_plane = from_behind(nodal_field[:, :, :1, :], "fluid", -1)
    widened = jnp.concatenate([nodal_field, top_plane], axis=2)
    row_part = from_behind(widened[:, :1], "struct", -1)
    return jnp.concatenate([widened, row_part], axis=1)


def fold_back(spread):
    count_y = spread.shape[1] - 1
    count_z = spread.shape[2] - 1
    row_part = from_behind(spread[:, count_y:], "struct", 1)
    folded = jnp.concatenate([spread[:, :1] + row_part, spread[:, 1:count_y]], axis=1)
    top_plane = from_behind(folded[:, :, count_z:], "fluid", 1)
    return jnp.concatenate([folded[:, :, :1] + top_plane, folded[:, :, 1:count_z]], axis=2)


def shards(shell_motion, owner, stencil_slot, stencil_weight, prev_motion, node_offset, cell_split):
    struct_count = lax.axis_size("struct")
    fluid_count = lax.axis_size("fluid")
    devices = struct_count * fluid_count
    capacity = 2 * shell_motion.shape[1] // devices
    targets = jnp.arange(devices, dtype=jnp.int32)
    owner_rows = owner[:, 0]
    onehot = (owner_rows[:, None] == targets[None, :]).astype(jnp.int32)
    before = jnp.cumsum(onehot, axis=0) - onehot
    slot_rank = jnp.sum(before * onehot, axis=1)
    slot_place = owner_rows * capacity + slot_rank
    packed = jnp.zeros((3, devices * capacity), jnp.float32).at[:, slot_place].set(shell_motion)
    received = lax.all_to_all(
        packed.reshape(3, devices, capacity),
        ("struct", "fluid"),
        split_axis=1,
        concat_axis=1,
        tiled=True,
    )
    received = received.reshape(3, devices * capacity)
    stencil_count, count_y, count_z, wall_width = stencil_slot.shape
    gathered = jnp.take(received, stencil_slot.reshape(-1), axis=1).reshape(
        3, stencil_count, count_y, count_z, wall_width
    )
    wall_values = jnp.sum(stencil_weight[None] * gathered, axis=1)
    motion = jnp.concatenate([wall_values, prev_motion[:, :, :, wall_width:]], axis=3)
    is_wall = (jnp.arange(motion.shape[3], dtype=jnp.int32) < wall_width)[None, None, None, :]
    masks = flip_masks(cell_split)
    offset_ext = upper_ghosts(node_offset)
    diagonal = fold_back(spread_sum(corner_diagonal(offset_ext, masks, count_y, count_z)))
    for sweep_index in range(SWEEPS):
        forces = fold_back(
            spread_sum(corner_forces(offset_ext, upper_ghosts(motion), masks, count_y, count_z))
        )
        motion = jnp.where(is_wall, motion, motion - RELAX_FACTOR * forces / diagonal)
    return motion


def solution(mesh):
    return jax.shard_map(
        shards,
        mesh=mesh,
        in_specs=(
            P(None, ("struct", "fluid")),
            P(("struct", "fluid"), None),
            P(None, "struct", "fluid", None),
            P(None, "struct", "fluid", None),
            P(None, "struct", "fluid", None),
            P(None, "struct", "fluid", None),
            P("struct", "fluid", None),
        ),
        out_specs=P(None, "struct", "fluid", None),
        check_vma=False,
    )
```

profile of v0, /device:TPU:0, one launch (start us, length us, event | category | flops | bytes accessed | tf_op | source)
XLA Modules:
  0.0 191.9 jit_solution(16414757542172310630)
XLA Ops:
  0.0 0.8 slice.619
  0.8 6.0 %collective-permute-start.2 = (f32[3,2,1,256]{3,2,1,0:T(1,128)S(1)}, f32[3,2,1,256]{3,2,1,0:T(1,128)S(1)}, u32[]{:S(2)}, u32[]{:S(2)}) collective-permute-start(f32[3,2,1,256]{3,2,1,0:T(1,128)S(1)} %slice.619), channel_id=1, source_target_pairs={{1,0},{2,1},{3,2},{4,3},{5,4},{6,5},{7,6},{8,7},{9,8},{10,9},{11,1... | collective-permute-start | bytes 18440 | tf_op jit(solution)/shard_map/ppermute | solution.py:19
  6.8 0.8 copy.1353
  7.7 1.1 fusion.2
  8.8 1.9 copy-done
  10.9 2.6 %broadcast_add_fusion = s32[128,64,128]{0,1,2:T(8,128)S(1)} fusion(s32[128,64,128]{0,1,2:T(8,128)} %copy-done, s32[128,64]{0,1:T(8,128)S(1)} %slice.845), kind=kLoop, calls=%fused_computation.12 | loop fusion | flops 1048576 | bytes 8421376 | tf_op jit(solution)/shard_map/reduce_window_sum
  13.5 2.4 %copy.1354 = s32[128,64,128]{0,2,1:T(8,128)S(1)} copy(s32[128,64,128]{0,1,2:T(8,128)S(1)} %broadcast_add_fusion) | data formatting | bytes 8388608 | tf_op jit(solution)/shard_map/reduce_window_sum
  16.0 2.8 %fusion.1 = s32[8192]{0:T(1024)S(1)} fusion(s32[128,64,128]{0,2,1:T(8,128)S(1)} %copy.1354, s32[8192]{0:T(1024)S(1)} %bitcast.86), kind=kLoop, calls=%fused_computation.4 | loop fusion | flops 5234688 | bytes 4259840 | tf_op jit(solution)/shard_map/reduce_sum | solution.py:186
  18.9 2.7 %copy.1355 = f32[8192,3]{1,0:T(8,128)} copy(f32[8192,3]{0,1:T(4,128)S(1)} %bitcast.88) | data formatting | bytes 196608 | tf_op args[0]
  21.5 24.5 %scatter_custom_fusion = f32[3,16384]{0,1:T(8,128)} fusion(s32[8192]{0:T(1024)S(1)} %bitcast.91, f32[8192,3]{1,0:T(8,128)} %copy.1355, f32[]{:T(128)} %constant.58.clone.1), kind=kCustom, calls=%fused_computation.10 | custom fusion | bytes 197120 | tf_op jit(solution)/shard_map/scatter | solution.py:188
  46.1 6.0 %copy.1356 = f32[3,128,128]{2,0,1:T(4,128)} copy(f32[3,128,128]{0,2,1:T(8,128)} %bitcast.81) | data formatting | bytes 393216 | tf_op jit(solution)/shard_map/reshape | solution.py:190
  52.0 5.2 %all-to-all-start = ((f32[3,128,128]{2,0,1:T(4,128)}), f32[3,128,128]{2,0,1:T(4,128)S(1)}, u32[]{:S(2)}, u32[]{:S(2)}) async-start(f32[3,128,128]{2,0,1:T(4,128)} %copy.1356), calls=%async_computation | async-start | bytes 524288 | tf_op jit(solution)/shard_map/all_to_all | solution.py:189
  57.6 2.2 %collective-permute-start.3 = (f32[3,1,9,256]{3,1,2,0:T(1,128)S(1)}, f32[3,1,9,256]{3,1,2,0:T(1,128)S(1)}, u32[]{:S(2)}, u32[]{:S(2)}) collective-permute-start(f32[3,1,9,256]{3,1,2,0:T(1,128)S(1)} %copy.1361), channel_id=1, source_target_pairs={{32,0},{64,32},{96,64},{0,96},{33,1},{65,33},{97,65},{1,97},{34,2}... | collective-permute-start | bytes 82952 | tf_op jit(solution)/shard_map/ppermute | solution.py:19
  60.0 2.0 %collective-permute-done.3 = f32[3,1,9,256]{3,1,2,0:T(1,128)S(1)} collective-permute-done((f32[3,1,9,256]{3,1,2,0:T(1,128)S(1)}, f32[3,1,9,256]{3,1,2,0:T(1,128)S(1)}, u32[]{:S(2)}, u32[]{:S(2)}) %collective-permute-start.3) | collective-permute-done | bytes 27680 | tf_op jit(solution)/shard_map/ppermute | solution.py:19
  62.5 5.5 %all-to-all-done = f32[3,128,128]{2,0,1:T(4,128)S(1)} async-done(((f32[3,128,128]{2,0,1:T(4,128)}), f32[3,128,128]{2,0,1:T(4,128)S(1)}, u32[]{:S(2)}, u32[]{:S(2)}) %all-to-all-start) | async-done | bytes 196640 | tf_op jit(solution)/shard_map/all_to_all | solution.py:189
  68.0 4.9 %copy.1357 = f32[3,128,128]{0,2,1:T(8,128)} copy(f32[3,128,128]{2,0,1:T(4,128)S(1)} %all-to-all-done) | data formatting | bytes 393216 | tf_op jit(solution)/shard_map/all_to_all | solution.py:189
  72.9 31.1 %gather_fusion = f32[8192,3]{1,0:T(8,128)} fusion(f32[3,16384]{0,1:T(8,128)} %bitcast.82, s32[8192]{0:T(1024)S(1)} %broadcast_clamp_fusion), kind=kCustom, calls=%fused_computation | custom fusion | bytes 229376 | tf_op jit(solution)/shard_map/jit(_take)/gather | solution.py:198
  104.0 6.1 %multiply_reduce_fusion = f32[3,2,8,128]{0,3,2,1:T(8,128)S(1)} fusion(f32[3,4,2,8,128]{0,4,3,2,1:T(8,128)} %bitcast.83, f32[4,2,8,128]{3,2,1,0:T(8,128)S(1)} %copy-done.5, pred[4,2,8,128]{3,2,1,0:T(8,128)(4,1)S(1)} %compare_and_fusion), kind=kLoop, calls=%fused_computation.5 | loop fusion | flops 67584 | bytes 163840 | tf_op jit(solution)/shard_map/reduce_sum | solution.py:201
  110.1 0.3 copy.1358
  110.5 0.9 collective-permute-start
  111.4 1.3 collective-permute-done
  112.8 1.5 collective-permute-start.1
  114.5 2.2 %collective-permute-done.1 = f32[3,1,9,256]{3,1,2,0:T(1,128)S(1)} collective-permute-done((f32[3,1,9,256]{3,1,2,0:T(1,128)S(1)}, f32[3,1,9,256]{3,1,2,0:T(1,128)S(1)}, u32[]{:S(2)}, u32[]{:S(2)}) %collective-permute-start.1) | collective-permute-done | bytes 27680 | tf_op jit(solution)/shard_map/ppermute | solution.py:19
  120.3 0.7 collective-permute-start.6
  121.3 1.3 collective-permute-start.4
  122.6 2.9 %collective-permute-done.6 = f32[3,1,9,256]{3,1,2,0:T(1,128)S(1)} collective-permute-done((f32[3,1,9,256]{3,1,2,0:T(1,128)S(1)}, f32[3,1,9,256]{3,1,2,0:T(1,128)S(1)}, u32[]{:S(2)}, u32[]{:S(2)}) %collective-permute-start.6) | collective-permute-done | bytes 27680 | tf_op jit(solution)/shard_map/ppermute | solution.py:19
  125.7 0.8 collective-permute-done.4
  126.7 5.3 %collective-permute-done.7 = f32[3,2,1,256]{3,1,2,0:T(2,128)S(1)} collective-permute-done((f32[3,2,1,256]{3,1,2,0:T(2,128)S(1)}, f32[3,2,1,256]{3,1,2,0:T(2,128)S(1)}, u32[]{:S(2)}, u32[]{:S(2)}) %collective-permute-start.7) | collective-permute-done | bytes 6176 | tf_op jit(solution)/shard_map/ppermute | solution.py:19
  132.1 1.0 collective-permute-done.5
  133.3 1.3 collective-permute-done.8
  134.6 1.4 collective-permute-start.9
  136.2 2.4 %collective-permute-done.9 = f32[3,1,9,256]{3,1,2,0:T(1,128)S(1)} collective-permute-done((f32[3,1,9,256]{3,1,2,0:T(1,128)S(1)}, f32[3,1,9,256]{3,1,2,0:T(1,128)S(1)}, u32[]{:S(2)}, u32[]{:S(2)}) %collective-permute-start.9) | collective-permute-done | bytes 27680 | tf_op jit(solution)/shard_map/ppermute | solution.py:19
  140.4 0.2 fusion.15
  140.7 0.3 collective-permute-start.10
  141.0 4.8 %collective-permute-done.10 = f32[3,1,9,256]{3,1,2,0:T(1,128)S(1)} collective-permute-done((f32[3,1,9,256]{3,1,2,0:T(1,128)S(1)}, f32[3,1,9,256]{3,1,2,0:T(1,128)S(1)}, u32[]{:S(2)}, u32[]{:S(2)}) %collective-permute-start.10) | collective-permute-done | bytes 27680 | tf_op jit(solution)/shard_map/ppermute | solution.py:19
  146.1 6.3 %collective-permute-done.11 = f32[3,2,1,256]{3,1,2,0:T(2,128)S(1)} collective-permute-done((f32[3,2,1,256]{3,1,2,0:T(2,128)S(1)}, f32[3,2,1,256]{3,1,2,0:T(2,128)S(1)}, u32[]{:S(2)}, u32[]{:S(2)}) %collective-permute-start.11) | collective-permute-done | bytes 6176 | tf_op jit(solution)/shard_map/ppermute | solution.py:19
  152.6 1.3 collective-permute-done.12
  153.9 1.4 collective-permute-start.13
  155.5 2.4 %collective-permute-done.13 = f32[3,1,9,256]{3,1,2,0:T(1,128)S(1)} collective-permute-done((f32[3,1,9,256]{3,1,2,0:T(1,128)S(1)}, f32[3,1,9,256]{3,1,2,0:T(1,128)S(1)}, u32[]{:S(2)}, u32[]{:S(2)}) %collective-permute-start.13) | collective-permute-done | bytes 27680 | tf_op jit(solution)/shard_map/ppermute | solution.py:19
  160.1 5.1 %collective-permute-done.14 = f32[3,1,9,256]{3,1,2,0:T(1,128)S(1)} collective-permute-done((f32[3,1,9,256]{3,1,2,0:T(1,128)S(1)}, f32[3,1,9,256]{3,1,2,0:T(1,128)S(1)}, u32[]{:S(2)}, u32[]{:S(2)}) %collective-permute-start.14) | collective-permute-done | bytes 27680 | tf_op jit(solution)/shard_map/ppermute | solution.py:19
  165.3 0.3 collective-permute-start.15
  165.6 6.3 %collective-permute-done.15 = f32[3,2,1,256]{3,1,2,0:T(2,128)S(1)} collective-permute-done((f32[3,2,1,256]{3,1,2,0:T(2,128)S(1)}, f32[3,2,1,256]{3,1,2,0:T(2,128)S(1)}, u32[]{:S(2)}, u32[]{:S(2)}) %collective-permute-start.15) | collective-permute-done | bytes 6176 | tf_op jit(solution)/shard_map/ppermute | solution.py:19
  172.1 1.3 collective-permute-done.16
  173.5 1.4 collective-permute-start.17
  175.0 2.4 %collective-permute-done.17 = f32[3,1,9,256]{3,1,2,0:T(1,128)S(1)} collective-permute-done((f32[3,1,9,256]{3,1,2,0:T(1,128)S(1)}, f32[3,1,9,256]{3,1,2,0:T(1,128)S(1)}, u32[]{:S(2)}, u32[]{:S(2)}) %collective-permute-start.17) | collective-permute-done | bytes 27680 | tf_op jit(solution)/shard_map/ppermute | solution.py:19
  179.6 5.1 %collective-permute-done.18 = f32[3,1,9,256]{3,1,2,0:T(1,128)S(1)} collective-permute-done((f32[3,1,9,256]{3,1,2,0:T(1,128)S(1)}, f32[3,1,9,256]{3,1,2,0:T(1,128)S(1)}, u32[]{:S(2)}, u32[]{:S(2)}) %collective-permute-start.18) | collective-permute-done | bytes 27680 | tf_op jit(solution)/shard_map/ppermute | solution.py:19
  184.9 6.3 %collective-permute-done.19 = f32[3,2,1,256]{3,1,2,0:T(2,128)S(1)} collective-permute-done((f32[3,2,1,256]{3,1,2,0:T(2,128)S(1)}, f32[3,2,1,256]{3,1,2,0:T(2,128)S(1)}, u32[]{:S(2)}, u32[]{:S(2)}) %collective-permute-start.19) | collective-permute-done | bytes 6176 | tf_op jit(solution)/shard_map/ppermute | solution.py:19
  191.3 0.7 subtract_select_fusion
  (307 shorter events, 12.1 us)
Async XLA Ops:
  0.8 56.7 %collective-permute-start.2 = (f32[3,2,1,256]{3,2,1,0:T(1,128)S(1)}, f32[3,2,1,256]{3,2,1,0:T(1,128)S(1)}, u32[]{:S(2)}, u32[]{:S(2)}) collective-permute-start(f32[3,2,1,256]{3,2,1,0:T(1,128)S(1)} %slice.619), channel_id=1, source_target_pairs={{1,0},{2,1},{3,2},{4,3},{5,4},{6,5},{7,6},{8,7},{9,8},{10,9},{11,1... | collective-permute-start | bytes 18440 | tf_op jit(solution)/shard_map/ppermute | solution.py:19
  8.8 1.9 %copy-start = (s32[128,64,128]{0,1,2:T(8,128)}, s32[128,64,128]{0,1,2:T(8,128)S(1)}, u32[]{:S(2)}) copy-start(s32[128,64,128]{0,1,2:T(8,128)S(1)} %fusion.2) | copy-start | bytes 12582916
  13.5 2.5 %copy-start.2 = (s32[8192,1]{0,1:T(1,128)S(1)}, s32[8192,1]{0,1:T(1,128)}, u32[]{:S(2)}) copy-start(s32[8192,1]{0,1:T(1,128)} %param.8) | copy-start | bytes 98308
  15.9 2.9 %copy-start.3 = (f32[3,8192]{1,0:T(4,128)S(1)}, f32[3,8192]{1,0:T(4,128)}, u32[]{:S(2)}) copy-start(f32[3,8192]{1,0:T(4,128)} %param.7) | copy-start | bytes 294916
  46.1 11.2 %copy-start.6 = (s32[2,8,256]{2,1,0:T(8,128)S(1)}, s32[2,8,256]{2,1,0:T(8,128)}, u32[]{:S(2)}) copy-start(s32[2,8,256]{2,1,0:T(8,128)} %param.13) | copy-start | bytes 49156
  46.1 11.3 %copy-start.4 = (s32[4,2,8,128]{3,2,1,0:T(8,128)S(1)}, s32[4,2,8,128]{3,2,1,0:T(8,128)}, u32[]{:S(2)}) copy-start(s32[4,2,8,128]{3,2,1,0:T(8,128)} %param.9) | copy-start | bytes 98308
  46.1 11.4 %copy-start.1 = (f32[3,2,8,256]{3,2,1,0:T(8,128)S(1)}, f32[3,2,8,256]{3,2,1,0:T(8,128)}, u32[]{:S(2)}) copy-start(f32[3,2,8,256]{3,2,1,0:T(8,128)} %param.12) | copy-start | bytes 147460
  46.1 13.9 %copy-start.7 = (f32[3,2,8,256]{3,2,1,0:T(8,128)S(1)}, f32[3,2,8,256]{3,2,1,0:T(8,128)}, u32[]{:S(2)}) copy-start(f32[3,2,8,256]{3,2,1,0:T(8,128)} %param.11) | copy-start | bytes 147460
  52.0 16.0 %all-to-all-start = ((f32[3,128,128]{2,0,1:T(4,128)}), f32[3,128,128]{2,0,1:T(4,128)S(1)}, u32[]{:S(2)}, u32[]{:S(2)}) async-start(f32[3,128,128]{2,0,1:T(4,128)} %copy.1356), calls=%async_computation | async-start | bytes 524288 | tf_op jit(solution)/shard_map/all_to_all | solution.py:189
  57.6 4.4 %collective-permute-start.3 = (f32[3,1,9,256]{3,1,2,0:T(1,128)S(1)}, f32[3,1,9,256]{3,1,2,0:T(1,128)S(1)}, u32[]{:S(2)}, u32[]{:S(2)}) collective-permute-start(f32[3,1,9,256]{3,1,2,0:T(1,128)S(1)} %copy.1361), channel_id=1, source_target_pairs={{32,0},{64,32},{96,64},{0,96},{33,1},{65,33},{97,65},{1,97},{34,2}... | collective-permute-start | bytes 82952 | tf_op jit(solution)/shard_map/ppermute | solution.py:19
  62.5 41.5 %copy-start.5 = (f32[4,2,8,128]{3,2,1,0:T(8,128)S(1)}, f32[4,2,8,128]{3,2,1,0:T(8,128)}, u32[]{:S(2)}) copy-start(f32[4,2,8,128]{3,2,1,0:T(8,128)} %param.10) | copy-start | bytes 98308
  110.5 2.3 %collective-permute-start = (f32[3,2,1,256]{3,2,1,0:T(1,128)S(1)}, f32[3,2,1,256]{3,2,1,0:T(1,128)S(1)}, u32[]{:S(2)}, u32[]{:S(2)}) collective-permute-start(f32[3,2,1,256]{3,2,1,0:T(1,128)S(1)} %fusion.199), channel_id=1, source_target_pairs={{1,0},{2,1},{3,2},{4,3},{5,4},{6,5},{7,6},{8,7},{9,8},{10,9},{11,1... | collective-permute-start | bytes 18440 | tf_op jit(solution)/shard_map/ppermute | solution.py:19
  112.8 3.9 %collective-permute-start.1 = (f32[3,1,9,256]{3,1,2,0:T(1,128)S(1)}, f32[3,1,9,256]{3,1,2,0:T(1,128)S(1)}, u32[]{:S(2)}, u32[]{:S(2)}) collective-permute-start(f32[3,1,9,256]{3,1,2,0:T(1,128)S(1)} %copy.1359), channel_id=1, source_target_pairs={{32,0},{64,32},{96,64},{0,96},{33,1},{65,33},{97,65},{1,97},{34,2}... | collective-permute-start | bytes 82952 | tf_op jit(solution)/shard_map/ppermute | solution.py:19
  120.3 5.1 %collective-permute-start.6 = (f32[3,1,9,256]{3,1,2,0:T(1,128)S(1)}, f32[3,1,9,256]{3,1,2,0:T(1,128)S(1)}, u32[]{:S(2)}, u32[]{:S(2)}) collective-permute-start(f32[3,1,9,256]{3,1,2,0:T(1,128)S(1)} %copy.1370), channel_id=1, source_target_pairs={{96,0},{0,32},{32,64},{64,96},{97,1},{1,33},{33,65},{65,97},{98,2}... | collective-permute-start | bytes 82952 | tf_op jit(solution)/shard_map/ppermute | solution.py:19
  121.3 5.1 %collective-permute-start.4 = (f32[3,1,9,256]{3,1,2,0:T(1,128)S(1)}, f32[3,1,9,256]{3,1,2,0:T(1,128)S(1)}, u32[]{:S(2)}, u32[]{:S(2)}) collective-permute-start(f32[3,1,9,256]{3,1,2,0:T(1,128)S(1)} %copy.1364), channel_id=1, source_target_pairs={{96,0},{0,32},{32,64},{64,96},{97,1},{1,33},{33,65},{65,97},{98,2}... | collective-permute-start | bytes 82952 | tf_op jit(solution)/shard_map/ppermute | solution.py:19
  125.6 6.4 %collective-permute-start.7 = (f32[3,2,1,256]{3,1,2,0:T(2,128)S(1)}, f32[3,2,1,256]{3,1,2,0:T(2,128)S(1)}, u32[]{:S(2)}, u32[]{:S(2)}) collective-permute-start(f32[3,2,1,256]{3,1,2,0:T(2,128)S(1)} %pad_maximum_fusion.52), channel_id=1, source_target_pairs={{31,0},{0,1},{1,2},{2,3},{3,4},{4,5},{5,6},{6,7},{7,8},{8,9},{9,10... | collective-permute-start | bytes 18440 | tf_op jit(solution)/shard_map/ppermute | solution.py:19
  126.6 6.4 %collective-permute-start.5 = (f32[3,2,1,256]{3,1,2,0:T(2,128)S(1)}, f32[3,2,1,256]{3,1,2,0:T(2,128)S(1)}, u32[]{:S(2)}, u32[]{:S(2)}) collective-permute-start(f32[3,2,1,256]{3,1,2,0:T(2,128)S(1)} %pad_maximum_fusion.53), channel_id=1, source_target_pairs={{31,0},{0,1},{1,2},{2,3},{3,4},{4,5},{5,6},{6,7},{7,8},{8,9},{9,10... | collective-permute-start | bytes 18440 | tf_op jit(solution)/shard_map/ppermute | solution.py:19
  133.2 1.4 collective-permute-start.8
  134.6 3.9 %collective-permute-start.9 = (f32[3,1,9,256]{3,1,2,0:T(1,128)S(1)}, f32[3,1,9,256]{3,1,2,0:T(1,128)S(1)}, u32[]{:S(2)}, u32[]{:S(2)}) collective-permute-start(f32[3,1,9,256]{3,1,2,0:T(1,128)S(1)} %copy.1376), channel_id=1, source_target_pairs={{32,0},{64,32},{96,64},{0,96},{33,1},{65,33},{97,65},{1,97},{34,2}... | collective-permute-start | bytes 82952 | tf_op jit(solution)/shard_map/ppermute | solution.py:19
  140.7 5.1 %collective-permute-start.10 = (f32[3,1,9,256]{3,1,2,0:T(1,128)S(1)}, f32[3,1,9,256]{3,1,2,0:T(1,128)S(1)}, u32[]{:S(2)}, u32[]{:S(2)}) collective-permute-start(f32[3,1,9,256]{3,1,2,0:T(1,128)S(1)} %copy.1378), channel_id=1, source_target_pairs={{96,0},{0,32},{32,64},{64,96},{97,1},{1,33},{33,65},{65,97},{98,2}... | collective-permute-start | bytes 82952 | tf_op jit(solution)/shard_map/ppermute | solution.py:19
  146.0 6.4 %collective-permute-start.11 = (f32[3,2,1,256]{3,1,2,0:T(2,128)S(1)}, f32[3,2,1,256]{3,1,2,0:T(2,128)S(1)}, u32[]{:S(2)}, u32[]{:S(2)}) collective-permute-start(f32[3,2,1,256]{3,1,2,0:T(2,128)S(1)} %pad_maximum_fusion.51), channel_id=1, source_target_pairs={{31,0},{0,1},{1,2},{2,3},{3,4},{4,5},{5,6},{6,7},{7,8},{8,9},{9,10... | collective-permute-start | bytes 18440 | tf_op jit(solution)/shard_map/ppermute | solution.py:19
  152.5 1.4 collective-permute-start.12
  153.9 3.9 %collective-permute-start.13 = (f32[3,1,9,256]{3,1,2,0:T(1,128)S(1)}, f32[3,1,9,256]{3,1,2,0:T(1,128)S(1)}, u32[]{:S(2)}, u32[]{:S(2)}) collective-permute-start(f32[3,1,9,256]{3,1,2,0:T(1,128)S(1)} %copy.1384), channel_id=1, source_target_pairs={{32,0},{64,32},{96,64},{0,96},{33,1},{65,33},{97,65},{1,97},{34,2}... | collective-permute-start | bytes 82952 | tf_op jit(solution)/shard_map/ppermute | solution.py:19
  160.0 5.1 %collective-permute-start.14 = (f32[3,1,9,256]{3,1,2,0:T(1,128)S(1)}, f32[3,1,9,256]{3,1,2,0:T(1,128)S(1)}, u32[]{:S(2)}, u32[]{:S(2)}) collective-permute-start(f32[3,1,9,256]{3,1,2,0:T(1,128)S(1)} %copy.1386), channel_id=1, source_target_pairs={{96,0},{0,32},{32,64},{64,96},{97,1},{1,33},{33,65},{65,97},{98,2}... | collective-permute-start | bytes 82952 | tf_op jit(solution)/shard_map/ppermute | solution.py:19
  165.3 6.7 %collective-permute-start.15 = (f32[3,2,1,256]{3,1,2,0:T(2,128)S(1)}, f32[3,2,1,256]{3,1,2,0:T(2,128)S(1)}, u32[]{:S(2)}, u32[]{:S(2)}) collective-permute-start(f32[3,2,1,256]{3,1,2,0:T(2,128)S(1)} %pad_maximum_fusion.50), channel_id=1, source_target_pairs={{31,0},{0,1},{1,2},{2,3},{3,4},{4,5},{5,6},{6,7},{7,8},{8,9},{9,10... | collective-permute-start | bytes 18440 | tf_op jit(solution)/shard_map/ppermute | solution.py:19
  172.0 1.4 collective-permute-start.16
  173.5 3.9 %collective-permute-start.17 = (f32[3,1,9,256]{3,1,2,0:T(1,128)S(1)}, f32[3,1,9,256]{3,1,2,0:T(1,128)S(1)}, u32[]{:S(2)}, u32[]{:S(2)}) collective-permute-start(f32[3,1,9,256]{3,1,2,0:T(1,128)S(1)} %copy.1392), channel_id=1, source_target_pairs={{32,0},{64,32},{96,64},{0,96},{33,1},{65,33},{97,65},{1,97},{34,2}... | collective-permute-start | bytes 82952 | tf_op jit(solution)/shard_map/ppermute | solution.py:19
  179.5 5.1 %collective-permute-start.18 = (f32[3,1,9,256]{3,1,2,0:T(1,128)S(1)}, f32[3,1,9,256]{3,1,2,0:T(1,128)S(1)}, u32[]{:S(2)}, u32[]{:S(2)}) collective-permute-start(f32[3,1,9,256]{3,1,2,0:T(1,128)S(1)} %copy.1394), channel_id=1, source_target_pairs={{96,0},{0,32},{32,64},{64,96},{97,1},{1,33},{33,65},{65,97},{98,2}... | collective-permute-start | bytes 82952 | tf_op jit(solution)/shard_map/ppermute | solution.py:19
  184.8 6.4 %collective-permute-start.19 = (f32[3,2,1,256]{3,1,2,0:T(2,128)S(1)}, f32[3,2,1,256]{3,1,2,0:T(2,128)S(1)}, u32[]{:S(2)}, u32[]{:S(2)}) collective-permute-start(f32[3,2,1,256]{3,1,2,0:T(2,128)S(1)} %pad_maximum_fusion.49), channel_id=1, source_target_pairs={{31,0},{0,1},{1,2},{2,3},{3,4},{4,5},{5,6},{6,7},{7,8},{8,9},{9,10... | collective-permute-start | bytes 18440 | tf_op jit(solution)/shard_map/ppermute | solution.py:19
where the time goes:
time: 192 us
  local copies, waits for them, and re-layouts  78.6 us (41%)
  waiting for transfers between devices  66 us (34%)
  starting transfers between devices  23.5 us (12%)
  other arithmetic  21.9 us (11%)
    ppermute x20, waiting for transfers between devices, from_behind(): return lax.ppermute(block, axis, route)  60.4 us
    gather x1, local copies, waits for them, and re-layouts, shards(): jnp.take(received, stencil_slot.reshape(-1), axis=1)  31.1 us
    scatter x1, local copies, waits for them, and re-layouts, shards(): jnp.zeros((3, devices * capacity), jnp.float32).at[:, slot_place]  24.5 us
    ppermute x20, starting transfers between devices, from_behind(): return lax.ppermute(block, axis, route)  18.3 us
    reduce_sum x1, other arithmetic, shards(): wall_values = jnp.sum(stencil_weight[None] * gathered, axis=1)  6.12 us
    reshape x1, local copies, waits for them, and re-layouts, shards(): packed.reshape(3, devices, capacity)  5.95 us
    all_to_all x1, waiting for transfers between devices, shards(): lax.all_to_all(packed.reshape(3, devices, capacity), ('struct', 'fluid'),...  5.54 us
    all_to_all x1, starting transfers between devices, shards(): lax.all_to_all(packed.reshape(3, devices, capacity), ('struct', 'fluid'),...  5.25 us
  transfers between devices with their start and end apart: 21, of which 20 were waited for; matrix products, arithmetic and copies ran while one was open for 24% of the time, Pallas kernels for 0%

commit v1 on v0

--- a/solution.py
+++ b/solution.py
@@ -186,12 +186,18 @@
     slot_rank = jnp.sum(before * onehot, axis=1)
     slot_place = owner_rows * capacity + slot_rank
     packed = jnp.zeros((3, devices * capacity), jnp.float32).at[:, slot_place].set(shell_motion)
-    received = lax.all_to_all(
-        packed.reshape(3, devices, capacity),
-        ("struct", "fluid"),
-        split_axis=1,
-        concat_axis=1,
-        tiled=True,
+    received = jnp.concatenate(
+        lax.all_to_all(
+            jnp.stack(
+                jnp.split(
+                    packed.reshape(3, devices, capacity), lax.axis_size(("struct", "fluid")), axis=1
+                )
+            ),
+            ("struct", "fluid"),
+            0,
+            0,
+        ),
+        axis=1,
     )
     received = received.reshape(3, devices * capacity)
     stencil_count, count_y, count_z, wall_width = stencil_slot.shape

time: 192 us -> 331 us (1.72); the launches traced: 192 us -> 326 us
  local copies, waits for them, and re-layouts: 78.6 us -> 208 us
  starting transfers between devices: 23.5 us -> 36.8 us
  waiting for transfers between devices: 66 us -> 55.5 us
    unnamed x18 -> x144, local copies, waits for them, and re-layouts: 4.61 us -> 119 us
    split x0 -> x7, local copies, waits for them, and re-layouts: none -> 13.7 us  [shards(): jnp.split(packed.reshape(3, devices, capacity), lax.axis_size(('struct',...]
    another operation x3 -> x5, local copies, waits for them, and re-layouts: 2.44 us -> 11.5 us  [the longest x2 9.08 us: shards(): jnp.stack(jnp.split(packed.reshape(3, devices, capacity), lax.axis_size((...]
    ppermute x20, starting transfers between devices: 18.3 us -> 25.7 us  [from_behind(): return lax.ppermute(block, axis, route)]
    all_to_all x1, starting transfers between devices: 5.25 us -> 11.1 us  [shards(): lax.all_to_all(jnp.stack(jnp.split(packed.reshape(3, devices, capacity),...]
    all_to_all x1, waiting for transfers between devices: 5.54 us -> 0.01 us  [shards(): lax.all_to_all(jnp.stack(jnp.split(packed.reshape(3, devices, capacity),...]
    ppermute x20, waiting for transfers between devices: 60.4 us -> 55.5 us  [from_behind(): return lax.ppermute(block, axis, route)]
    all_to_all x1 -> x0, local copies, waits for them, and re-layouts: 4.86 us -> none  [shards(): lax.all_to_all(packed.reshape(3, devices, capacity), ('struct', 'fluid'),...]
  transfers between devices with their start and end apart: 21 -> 21, of which waited for: 20 -> 19; matrix products, arithmetic and copies ran while one was open for 24% -> 1% of each run, Pallas kernels for 0% -> 0%
where the time goes in v1:
time: 331 us; the launch traced here: 326 us
  local copies, waits for them, and re-layouts  208 us (63%)
  waiting for transfers between devices  55.5 us (17%)
  starting transfers between devices  36.8 us (11%)
  other arithmetic  23.5 us (7%)
    unnamed x144, local copies, waits for them, and re-layouts  119 us
    ppermute x20, waiting for transfers between devices, from_behind(): return lax.ppermute(block, axis, route)  55.5 us
    gather x1, local copies, waits for them, and re-layouts, shards(): jnp.take(received, stencil_slot.reshape(-1), axis=1)  31.1 us
    ppermute x20, starting transfers between devices, from_behind(): return lax.ppermute(block, axis, route)  25.7 us
    scatter x1, local copies, waits for them, and re-layouts, shards(): jnp.zeros((3, devices * capacity), jnp.float32).at[:, slot_place]  24.5 us
    split x7, local copies, waits for them, and re-layouts, shards(): jnp.split(packed.reshape(3, devices, capacity), lax.axis_size(('struct',...  13.7 us
    all_to_all x1, starting transfers between devices, shards(): lax.all_to_all(jnp.stack(jnp.split(packed.reshape(3, devices, capacity),...  11.1 us
    another operation x2, local copies, waits for them, and re-layouts, shards(): jnp.stack(jnp.split(packed.reshape(3, devices, capacity), lax.axis_size((...  9.08 us
  transfers between devices with their start and end apart: 21, of which 19 were waited for; matrix products, arithmetic and copies ran while one was open for 1% of the time, Pallas kernels for 0%

profile of v1, /device:TPU:0, one launch (start us, length us, event | category | flops | bytes accessed | tf_op | source)
XLA Modules:
  0.0 326.2 jit_solution(17515380364196647504)
XLA Ops:
  2.0 1.9 copy-done
  4.0 2.6 broadcast_add_fusion
  6.7 2.4 copy.1994
  9.1 2.8 fusion.1
  12.1 2.7 copy.1995
  14.7 24.5 %scatter_custom_fusion = f32[3,16384]{0,1:T(8,128)} fusion(s32[8192]{0:T(1024)S(1)} %bitcast.227, f32[8192,3]{1,0:T(8,128)} %copy.1995, f32[]{:T(128)} %constant.58.clone.1), kind=kCustom, calls=%fused_computation.10 | custom fusion | bytes 197120 | tf_op jit(solution)/shard_map/scatter | solution.py:188
  39.3 2.4 fusion.248
  41.6 2.4 fusion.247
  44.0 2.4 fusion.252
  46.4 2.5 fusion.251
  56.6 1.5 copy.2263
  65.5 1.5 copy.2269
  67.0 1.5 copy.2270
  83.4 1.5 copy.2281
  87.9 1.5 copy.2284
  95.3 1.5 copy.2289
  99.8 1.5 copy.2292
  104.2 1.5 copy.2295
  111.6 1.5 copy.2186
  116.1 1.5 copy.2189
  130.9 1.5 copy.2199
  138.3 1.5 copy.2204
  154.7 1.5 copy.2215
  159.2 1.5 copy.2218
  167.0 8.2 %stack.432 = f32[128,3,1,128]{3,0,2,1:T(8,128)S(1)} concatenate(f32[1,3,1,128]{3,0,2,1:T(1,128)S(1)} %bitcast.355, f32[1,3,1,128]{3,0,2,1:T(1,128)S(1)} %bitcast.342, f32[1,3,1,128]{3,0,2,1:T(1,128)S(1)} %bitcast.343, f32[1,3,1,128]{3,0,2,1:T(1,128)S(1)} %bitcast.344, f32[1,3,1,128]{3,0,2,1:T(1,128)S(1)} %bitcast.345, f32[1,3,1,128]{3,0,2,1:T(1,128)S(1)} %bitcast.346, ...), dimensions={0} | concatenate | bytes 393216 | tf_op jit(solution)/shard_map/stack | solution.py:191
  176.1 11.1 %all-to-all-start = ((f32[128,3,1,128]{3,2,1,0:T(1,128)}), f32[128,3,1,128]{3,2,1,0:T(1,128)S(1)}, u32[]{:S(2)}, u32[]{:S(2)}) async-start(f32[128,3,1,128]{3,2,1,0:T(1,128)} %copy.2124), calls=%async_computation | async-start | bytes 393216 | tf_op jit(solution)/shard_map/all_to_all | solution.py:190
  187.3 5.0 %collective-permute-start.2 = (f32[3,2,1,256]{3,2,1,0:T(1,128)S(1)}, f32[3,2,1,256]{3,2,1,0:T(1,128)S(1)}, u32[]{:S(2)}, u32[]{:S(2)}) collective-permute-start(f32[3,2,1,256]{3,2,1,0:T(1,128)S(1)} %slice.619), channel_id=1, source_target_pairs={{1,0},{2,1},{3,2},{4,3},{5,4},{6,5},{7,6},{8,7},{9,8},{10,9},{11,1... | collective-permute-start | bytes 18440 | tf_op jit(solution)/shard_map/ppermute | solution.py:19
  194.0 2.8 collective-permute-start.3
  198.9 4.7 %copy.2125 = f32[3,128,1,128]{0,3,1,2:T(8,128)} copy(f32[3,128,1,128]{3,2,0,1:T(1,128)S(1)} %bitcast.220) | data formatting | bytes 393216 | tf_op jit(solution)/shard_map/reshape | solution.py:189
  203.6 31.1 %gather_fusion = f32[8192,3]{1,0:T(8,128)} fusion(f32[3,16384]{0,1:T(8,128)} %bitcast.217, s32[8192]{0:T(1024)S(1)} %broadcast_clamp_fusion), kind=kCustom, calls=%fused_computation | custom fusion | bytes 229376 | tf_op jit(solution)/shard_map/jit(_take)/gather | solution.py:204
  234.7 6.1 %multiply_reduce_fusion = f32[3,2,8,128]{0,3,2,1:T(8,128)S(1)} fusion(f32[3,4,2,8,128]{0,4,3,2,1:T(8,128)} %bitcast.218, f32[4,2,8,128]{3,2,1,0:T(8,128)S(1)} %copy-done.4, pred[4,2,8,128]{3,2,1,0:T(8,128)(4,1)S(1)} %compare_and_fusion), kind=kLoop, calls=%fused_computation.5 | loop fusion | flops 67584 | bytes 163840 | tf_op jit(solution)/shard_map/reduce_sum | solution.py:207
  241.2 3.9 %collective-permute-start = (f32[3,2,1,256]{3,2,1,0:T(1,128)S(1)}, f32[3,2,1,256]{3,2,1,0:T(1,128)S(1)}, u32[]{:S(2)}, u32[]{:S(2)}) collective-permute-start(f32[3,2,1,256]{3,2,1,0:T(1,128)S(1)} %fusion.199), channel_id=1, source_target_pairs={{1,0},{2,1},{3,2},{4,3},{5,4},{6,5},{7,6},{8,7},{9,8},{10,9},{11,1... | collective-permute-start | bytes 18440 | tf_op jit(solution)/shard_map/ppermute | solution.py:19
  246.5 3.3 %collective-permute-start.1 = (f32[3,1,9,256]{3,1,2,0:T(1,128)S(1)}, f32[3,1,9,256]{3,1,2,0:T(1,128)S(1)}, u32[]{:S(2)}, u32[]{:S(2)}) collective-permute-start(f32[3,1,9,256]{3,1,2,0:T(1,128)S(1)} %copy.2127), channel_id=1, source_target_pairs={{32,0},{64,32},{96,64},{0,96},{33,1},{65,33},{97,65},{1,97},{34,2}... | collective-permute-start | bytes 82952 | tf_op jit(solution)/shard_map/ppermute | solution.py:19
  255.3 2.0 collective-permute-start.4
  257.3 3.1 collective-permute-done.6
  261.2 5.7 %collective-permute-done.7 = f32[3,2,1,256]{3,1,2,0:T(2,128)S(1)} collective-permute-done((f32[3,2,1,256]{3,1,2,0:T(2,128)S(1)}, f32[3,2,1,256]{3,1,2,0:T(2,128)S(1)}, u32[]{:S(2)}, u32[]{:S(2)}) %collective-permute-start.7) | collective-permute-done | bytes 6176 | tf_op jit(solution)/shard_map/ppermute | solution.py:19
  269.1 2.1 collective-permute-start.9
  271.3 1.7 collective-permute-done.9
  276.6 3.7 %collective-permute-done.10 = f32[3,1,9,256]{3,1,2,0:T(1,128)S(1)} collective-permute-done((f32[3,1,9,256]{3,1,2,0:T(1,128)S(1)}, f32[3,1,9,256]{3,1,2,0:T(1,128)S(1)}, u32[]{:S(2)}, u32[]{:S(2)}) %collective-permute-start.10) | collective-permute-done | bytes 27680 | tf_op jit(solution)/shard_map/ppermute | solution.py:19
  280.6 6.3 %collective-permute-done.11 = f32[3,2,1,256]{3,1,2,0:T(2,128)S(1)} collective-permute-done((f32[3,2,1,256]{3,1,2,0:T(2,128)S(1)}, f32[3,2,1,256]{3,1,2,0:T(2,128)S(1)}, u32[]{:S(2)}, u32[]{:S(2)}) %collective-permute-start.11) | collective-permute-done | bytes 6176 | tf_op jit(solution)/shard_map/ppermute | solution.py:19
  288.4 2.1 collective-permute-start.13
  290.6 1.7 collective-permute-done.13
  294.7 4.9 %collective-permute-done.14 = f32[3,1,9,256]{3,1,2,0:T(1,128)S(1)} collective-permute-done((f32[3,1,9,256]{3,1,2,0:T(1,128)S(1)}, f32[3,1,9,256]{3,1,2,0:T(1,128)S(1)}, u32[]{:S(2)}, u32[]{:S(2)}) %collective-permute-start.14) | collective-permute-done | bytes 27680 | tf_op jit(solution)/shard_map/ppermute | solution.py:19
  299.9 6.3 %collective-permute-done.15 = f32[3,2,1,256]{3,1,2,0:T(2,128)S(1)} collective-permute-done((f32[3,2,1,256]{3,1,2,0:T(2,128)S(1)}, f32[3,2,1,256]{3,1,2,0:T(2,128)S(1)}, u32[]{:S(2)}, u32[]{:S(2)}) %collective-permute-start.15) | collective-permute-done | bytes 6176 | tf_op jit(solution)/shard_map/ppermute | solution.py:19
  307.7 2.1 collective-permute-start.17
  309.9 1.7 collective-permute-done.17
  313.9 5.1 %collective-permute-done.18 = f32[3,1,9,256]{3,1,2,0:T(1,128)S(1)} collective-permute-done((f32[3,1,9,256]{3,1,2,0:T(1,128)S(1)}, f32[3,1,9,256]{3,1,2,0:T(1,128)S(1)}, u32[]{:S(2)}, u32[]{:S(2)}) %collective-permute-start.18) | collective-permute-done | bytes 27680 | tf_op jit(solution)/shard_map/ppermute | solution.py:19
  319.2 6.3 %collective-permute-done.19 = f32[3,2,1,256]{3,1,2,0:T(2,128)S(1)} collective-permute-done((f32[3,2,1,256]{3,1,2,0:T(2,128)S(1)}, f32[3,2,1,256]{3,1,2,0:T(2,128)S(1)}, u32[]{:S(2)}, u32[]{:S(2)}) %collective-permute-start.19) | collective-permute-done | bytes 6176 | tf_op jit(solution)/shard_map/ppermute | solution.py:19
  (441 shorter events, 125.7 us)
Async XLA Ops:
  2.0 1.9 copy-start
  6.7 2.5 copy-start.2
  9.1 2.9 copy-start.3
  90.8 96.4 %copy-start.1 = (f32[3,2,8,256]{3,2,1,0:T(8,128)S(1)}, f32[3,2,8,256]{3,2,1,0:T(8,128)}, u32[]{:S(2)}) copy-start(f32[3,2,8,256]{3,2,1,0:T(8,128)} %param.12) | copy-start | bytes 147460
  95.3 98.6 %copy-start.5 = (s32[2,8,256]{2,1,0:T(8,128)S(1)}, s32[2,8,256]{2,1,0:T(8,128)}, u32[]{:S(2)}) copy-start(s32[2,8,256]{2,1,0:T(8,128)} %param.13) | copy-start | bytes 49156
  162.8 34.1 %copy-start.6 = (f32[3,2,8,256]{3,2,1,0:T(8,128)S(1)}, f32[3,2,8,256]{3,2,1,0:T(8,128)}, u32[]{:S(2)}) copy-start(f32[3,2,8,256]{3,2,1,0:T(8,128)} %param.11) | copy-start | bytes 147460
  176.1 22.8 %all-to-all-start = ((f32[128,3,1,128]{3,2,1,0:T(1,128)}), f32[128,3,1,128]{3,2,1,0:T(1,128)S(1)}, u32[]{:S(2)}, u32[]{:S(2)}) async-start(f32[128,3,1,128]{3,2,1,0:T(1,128)} %copy.2124), calls=%async_computation | async-start | bytes 393216 | tf_op jit(solution)/shard_map/all_to_all | solution.py:190
  187.3 6.6 %collective-permute-start.2 = (f32[3,2,1,256]{3,2,1,0:T(1,128)S(1)}, f32[3,2,1,256]{3,2,1,0:T(1,128)S(1)}, u32[]{:S(2)}, u32[]{:S(2)}) collective-permute-start(f32[3,2,1,256]{3,2,1,0:T(1,128)S(1)} %slice.619), channel_id=1, source_target_pairs={{1,0},{2,1},{3,2},{4,3},{5,4},{6,5},{7,6},{8,7},{9,8},{10,9},{11,1... | collective-permute-start | bytes 18440 | tf_op jit(solution)/shard_map/ppermute | solution.py:19
  194.0 4.3 %collective-permute-start.3 = (f32[3,1,9,256]{3,1,2,0:T(1,128)S(1)}, f32[3,1,9,256]{3,1,2,0:T(1,128)S(1)}, u32[]{:S(2)}, u32[]{:S(2)}) collective-permute-start(f32[3,1,9,256]{3,1,2,0:T(1,128)S(1)} %copy.2129), channel_id=1, source_target_pairs={{32,0},{64,32},{96,64},{0,96},{33,1},{65,33},{97,65},{1,97},{34,2}... | collective-permute-start | bytes 82952 | tf_op jit(solution)/shard_map/ppermute | solution.py:19
  198.9 35.8 %copy-start.4 = (f32[4,2,8,128]{3,2,1,0:T(8,128)S(1)}, f32[4,2,8,128]{3,2,1,0:T(8,128)}, u32[]{:S(2)}) copy-start(f32[4,2,8,128]{3,2,1,0:T(8,128)} %param.10) | copy-start | bytes 98308
  241.2 5.2 %collective-permute-start = (f32[3,2,1,256]{3,2,1,0:T(1,128)S(1)}, f32[3,2,1,256]{3,2,1,0:T(1,128)S(1)}, u32[]{:S(2)}, u32[]{:S(2)}) collective-permute-start(f32[3,2,1,256]{3,2,1,0:T(1,128)S(1)} %fusion.199), channel_id=1, source_target_pairs={{1,0},{2,1},{3,2},{4,3},{5,4},{6,5},{7,6},{8,7},{9,8},{10,9},{11,1... | collective-permute-start | bytes 18440 | tf_op jit(solution)/shard_map/ppermute | solution.py:19
  246.5 4.8 %collective-permute-start.1 = (f32[3,1,9,256]{3,1,2,0:T(1,128)S(1)}, f32[3,1,9,256]{3,1,2,0:T(1,128)S(1)}, u32[]{:S(2)}, u32[]{:S(2)}) collective-permute-start(f32[3,1,9,256]{3,1,2,0:T(1,128)S(1)} %copy.2127), channel_id=1, source_target_pairs={{32,0},{64,32},{96,64},{0,96},{33,1},{65,33},{97,65},{1,97},{34,2}... | collective-permute-start | bytes 82952 | tf_op jit(solution)/shard_map/ppermute | solution.py:19
  254.9 5.4 %collective-permute-start.6 = (f32[3,1,9,256]{3,1,2,0:T(1,128)S(1)}, f32[3,1,9,256]{3,1,2,0:T(1,128)S(1)}, u32[]{:S(2)}, u32[]{:S(2)}) collective-permute-start(f32[3,1,9,256]{3,1,2,0:T(1,128)S(1)} %copy.2138), channel_id=1, source_target_pairs={{96,0},{0,32},{32,64},{64,96},{97,1},{1,33},{33,65},{65,97},{98,2}... | collective-permute-start | bytes 82952 | tf_op jit(solution)/shard_map/ppermute | solution.py:19
  255.3 5.6 %collective-permute-start.4 = (f32[3,1,9,256]{3,1,2,0:T(1,128)S(1)}, f32[3,1,9,256]{3,1,2,0:T(1,128)S(1)}, u32[]{:S(2)}, u32[]{:S(2)}) collective-permute-start(f32[3,1,9,256]{3,1,2,0:T(1,128)S(1)} %copy.2132), channel_id=1, source_target_pairs={{96,0},{0,32},{32,64},{64,96},{97,1},{1,33},{33,65},{65,97},{98,2}... | collective-permute-start | bytes 82952 | tf_op jit(solution)/shard_map/ppermute | solution.py:19
  260.5 6.4 %collective-permute-start.7 = (f32[3,2,1,256]{3,1,2,0:T(2,128)S(1)}, f32[3,2,1,256]{3,1,2,0:T(2,128)S(1)}, u32[]{:S(2)}, u32[]{:S(2)}) collective-permute-start(f32[3,2,1,256]{3,1,2,0:T(2,128)S(1)} %pad_maximum_fusion.52), channel_id=1, source_target_pairs={{31,0},{0,1},{1,2},{2,3},{3,4},{4,5},{5,6},{6,7},{7,8},{8,9},{9,10... | collective-permute-start | bytes 18440 | tf_op jit(solution)/shard_map/ppermute | solution.py:19
  261.1 6.4 %collective-permute-start.5 = (f32[3,2,1,256]{3,1,2,0:T(2,128)S(1)}, f32[3,2,1,256]{3,1,2,0:T(2,128)S(1)}, u32[]{:S(2)}, u32[]{:S(2)}) collective-permute-start(f32[3,2,1,256]{3,1,2,0:T(2,128)S(1)} %pad_maximum_fusion.53), channel_id=1, source_target_pairs={{31,0},{0,1},{1,2},{2,3},{3,4},{4,5},{5,6},{6,7},{7,8},{8,9},{9,10... | collective-permute-start | bytes 18440 | tf_op jit(solution)/shard_map/ppermute | solution.py:19
  267.6 1.4 collective-permute-start.8
  269.1 3.9 %collective-permute-start.9 = (f32[3,1,9,256]{3,1,2,0:T(1,128)S(1)}, f32[3,1,9,256]{3,1,2,0:T(1,128)S(1)}, u32[]{:S(2)}, u32[]{:S(2)}) collective-permute-start(f32[3,1,9,256]{3,1,2,0:T(1,128)S(1)} %copy.2144), channel_id=1, source_target_pairs={{32,0},{64,32},{96,64},{0,96},{33,1},{65,33},{97,65},{1,97},{34,2}... | collective-permute-start | bytes 82952 | tf_op jit(solution)/shard_map/ppermute | solution.py:19
  275.2 5.1 %collective-permute-start.10 = (f32[3,1,9,256]{3,1,2,0:T(1,128)S(1)}, f32[3,1,9,256]{3,1,2,0:T(1,128)S(1)}, u32[]{:S(2)}, u32[]{:S(2)}) collective-permute-start(f32[3,1,9,256]{3,1,2,0:T(1,128)S(1)} %copy.2146), channel_id=1, source_target_pairs={{96,0},{0,32},{32,64},{64,96},{97,1},{1,33},{33,65},{65,97},{98,2}... | collective-permute-start | bytes 82952 | tf_op jit(solution)/shard_map/ppermute | solution.py:19
  280.4 6.4 %collective-permute-start.11 = (f32[3,2,1,256]{3,1,2,0:T(2,128)S(1)}, f32[3,2,1,256]{3,1,2,0:T(2,128)S(1)}, u32[]{:S(2)}, u32[]{:S(2)}) collective-permute-start(f32[3,2,1,256]{3,1,2,0:T(2,128)S(1)} %pad_maximum_fusion.51), channel_id=1, source_target_pairs={{31,0},{0,1},{1,2},{2,3},{3,4},{4,5},{5,6},{6,7},{7,8},{8,9},{9,10... | collective-permute-start | bytes 18440 | tf_op jit(solution)/shard_map/ppermute | solution.py:19
  287.0 1.4 collective-permute-start.12
  288.4 3.9 %collective-permute-start.13 = (f32[3,1,9,256]{3,1,2,0:T(1,128)S(1)}, f32[3,1,9,256]{3,1,2,0:T(1,128)S(1)}, u32[]{:S(2)}, u32[]{:S(2)}) collective-permute-start(f32[3,1,9,256]{3,1,2,0:T(1,128)S(1)} %copy.2152), channel_id=1, source_target_pairs={{32,0},{64,32},{96,64},{0,96},{33,1},{65,33},{97,65},{1,97},{34,2}... | collective-permute-start | bytes 82952 | tf_op jit(solution)/shard_map/ppermute | solution.py:19
  294.5 5.1 %collective-permute-start.14 = (f32[3,1,9,256]{3,1,2,0:T(1,128)S(1)}, f32[3,1,9,256]{3,1,2,0:T(1,128)S(1)}, u32[]{:S(2)}, u32[]{:S(2)}) collective-permute-start(f32[3,1,9,256]{3,1,2,0:T(1,128)S(1)} %copy.2154), channel_id=1, source_target_pairs={{96,0},{0,32},{32,64},{64,96},{97,1},{1,33},{33,65},{65,97},{98,2}... | collective-permute-start | bytes 82952 | tf_op jit(solution)/shard_map/ppermute | solution.py:19
  299.7 6.4 %collective-permute-start.15 = (f32[3,2,1,256]{3,1,2,0:T(2,128)S(1)}, f32[3,2,1,256]{3,1,2,0:T(2,128)S(1)}, u32[]{:S(2)}, u32[]{:S(2)}) collective-permute-start(f32[3,2,1,256]{3,1,2,0:T(2,128)S(1)} %pad_maximum_fusion.50), channel_id=1, source_target_pairs={{31,0},{0,1},{1,2},{2,3},{3,4},{4,5},{5,6},{6,7},{7,8},{8,9},{9,10... | collective-permute-start | bytes 18440 | tf_op jit(solution)/shard_map/ppermute | solution.py:19
  306.3 1.4 collective-permute-start.16
  307.7 3.9 %collective-permute-start.17 = (f32[3,1,9,256]{3,1,2,0:T(1,128)S(1)}, f32[3,1,9,256]{3,1,2,0:T(1,128)S(1)}, u32[]{:S(2)}, u32[]{:S(2)}) collective-permute-start(f32[3,1,9,256]{3,1,2,0:T(1,128)S(1)} %copy.2160), channel_id=1, source_target_pairs={{32,0},{64,32},{96,64},{0,96},{33,1},{65,33},{97,65},{1,97},{34,2}... | collective-permute-start | bytes 82952 | tf_op jit(solution)/shard_map/ppermute | solution.py:19
  313.8 5.1 %collective-permute-start.18 = (f32[3,1,9,256]{3,1,2,0:T(1,128)S(1)}, f32[3,1,9,256]{3,1,2,0:T(1,128)S(1)}, u32[]{:S(2)}, u32[]{:S(2)}) collective-permute-start(f32[3,1,9,256]{3,1,2,0:T(1,128)S(1)} %copy.2162), channel_id=1, source_target_pairs={{96,0},{0,32},{32,64},{64,96},{97,1},{1,33},{33,65},{65,97},{98,2}... | collective-permute-start | bytes 82952 | tf_op jit(solution)/shard_map/ppermute | solution.py:19
  319.0 6.4 %collective-permute-start.19 = (f32[3,2,1,256]{3,1,2,0:T(2,128)S(1)}, f32[3,2,1,256]{3,1,2,0:T(2,128)S(1)}, u32[]{:S(2)}, u32[]{:S(2)}) collective-permute-start(f32[3,2,1,256]{3,1,2,0:T(2,128)S(1)} %pad_maximum_fusion.49), channel_id=1, source_target_pairs={{31,0},{0,1},{1,2},{2,3},{3,4},{4,5},{5,6},{6,7},{7,8},{8,9},{9,10... | collective-permute-start | bytes 18440 | tf_op jit(solution)/shard_map/ppermute | solution.py:19
